TPU v7x, 32 devices: a whole 2x2x4 slice. The times are simulated.
32 devices in a mesh: gx: 4 (over y, core), gy: 2 (over x), gz: 4 (over z).
Axes of the slice: x: 2, y: 2, z: 4, core: 2. Of those that a mesh axis runs over, the one named last changes fastest.
Arguments:
- stem: bfloat16 [2, 4, 2, 4, 256, 1024], P(None, 'gx', 'gy', 'gz'), may hold values from -6 to 6
- branch_one: bfloat16 [2, 2, 1024, 1024], replicated, may hold values from -0.125 to 0.125
- branch_two: bfloat16 [2, 2, 1024, 1024], P(None, None, ('gy', 'gz')), may hold values from -0.1875 to 0.1875
- branch_three: bfloat16 [2, 2, 1024, 1024], P(None, None, 'gz'), may hold values from -0.125 to 0.125
- slice_values: int32 [3], replicated, may hold values from 0 to 1, as said below
Outputs:
- contracted: bfloat16 [2, 4, 2, 4, 256, 1024], P(None, 'gx', 'gy', 'gz')
Inputs may be any that keep to these rules, and one draw needn't show every extreme that they name: `slice_values`: the first two slices differ.
All inputs are finite; a program needn't handle non-finite values.
Results may differ from a plain program's by a relative error of at most 0.0057.
Values may be sent and summed in bfloat16 or wider, within the bound.
A program may use at most 128 MiB of HBM per device.

v0:
```python
import jax
import jax.numpy as jnp
from jax import lax
from jax.sharding import PartitionSpec as P

WIDTH = 1024
ROWS = 256


def complex_matrix(branch):
    top_half = jnp.concatenate([branch[0], branch[1]], axis=1)
    bottom_half = jnp.concatenate([-branch[1], branch[0]], axis=1)
    return jnp.concatenate([top_half, bottom_half], axis=0)


def complex_product(operand, branch):
    joined = jnp.concatenate([operand[0], operand[1]], axis=1)
    result = jnp.dot(joined, complex_matrix(branch), preferred_element_type=jnp.float32)
    columns = branch.shape[2]
    return jnp.stack([result[:, :columns], result[:, columns:]])


def split_result(result):
    columns = result.shape[1] // 2
    return jnp.stack([result[:, :columns], result[:, columns:]])


def make_accumulate(operand, shard_rows):
    real_part = operand[0]
    imag_part = operand[1]
    joined = jnp.concatenate([real_part, imag_part], axis=1)
    return jnp.dot(joined, complex_matrix(shard_rows), preferred_element_type=jnp.float32)


def third_contraction(operand, branch_three, slice_values):
    local_third = lax.dynamic_index_in_dim(branch_three, slice_values[2], 0, keepdims=False)
    summed = make_accumulate(operand, lax.all_gather(local_third, "gz", axis=1, tiled=True))
    return split_result(summed).astype(jnp.bfloat16)


def body(stem, branch_one, branch_two, branch_three, slice_values):
    count_gx = lax.axis_size("gx")
    count_gy = lax.axis_size("gy")
    count_gz = lax.axis_size("gz")
    group_one = count_gx * count_gy
    group_two = count_gy * count_gz
    rows_one = ROWS // group_one
    rows_two = ROWS // group_two
    part_one = WIDTH // group_one
    part_two = WIDTH // group_two
    first_branch = lax.dynamic_index_in_dim(branch_one, slice_values[0], 0, keepdims=False)
    arrived = lax.all_to_all(
        stem.reshape(2, 1, group_one, rows_one, WIDTH),
        ("gx", "gy"),
        split_axis=2,
        concat_axis=1,
        tiled=True,
    )
    ordered = arrived.reshape(2, group_one, rows_one, part_one, group_one).transpose(0, 2, 4, 1, 3)
    ordered = ordered.reshape(2, ROWS, WIDTH)
    middle = complex_product(ordered, first_branch).astype(jnp.bfloat16)
    gathered = lax.all_to_all(
        middle.reshape(2, group_two, 1, rows_two, WIDTH),
        ("gy", "gz"),
        split_axis=1,
        concat_axis=2,
        tiled=True,
    )
    regrouped = gathered.reshape(2, group_two, rows_two, part_two, group_two).transpose(
        0, 2, 4, 1, 3
    )
    regrouped = regrouped.reshape(2, ROWS, WIDTH)
    local_second = lax.dynamic_index_in_dim(branch_two, slice_values[1], 0, keepdims=False)
    summed = make_accumulate(
        regrouped, lax.all_gather(local_second, ("gy", "gz"), axis=1, tiled=True)
    )
    second = split_result(summed).astype(jnp.bfloat16)
    returned = lax.all_to_all(
        second.reshape(2, 1, rows_two, group_two, group_two, part_two),
        ("gy", "gz"),
        split_axis=4,
        concat_axis=1,
        tiled=True,
    )
    result = third_contraction(returned.reshape(2, ROWS, WIDTH), branch_three, slice_values)
    return result.reshape(stem.shape)


def solution(mesh):
    return jax.shard_map(
        body,
        mesh=mesh,
        in_specs=(
            P(None, "gx", "gy", "gz", None, None),
            P(),
            P(None, None, ("gy", "gz"), None),
            P(None, None, "gz", None),
            P(),
        ),
        out_specs=P(None, "gx", "gy", "gz", None, None),
        check_vma=False,
    )
```

profile of v0, /device:TPU:5, one launch (start us, length us, event | category | flops | bytes accessed | tf_op | source)
XLA Modules:
  0.0 248.9 jit_solution(15021778729917147188)
XLA Ops:
  6.5 0.0 copy-start
  6.5 1.4 fusion.52
  9.9 1.9 constant_dynamic-slice_fusion.1
  11.8 0.0 all-gather.5.cloned.1.call-update
  11.8 1.1 copy.38
  13.0 4.5 %all-to-all-start = ((bf16[2,1,8,32,1024]{4,3,1,0,2:T(8,128)(2,1)}), bf16[2,1,8,32,1024]{4,3,1,0,2:T(8,128)(2,1)S(1)}, u32[]{:S(2)}, u32[]{:S(2)}) async-start(bf16[2,1,8,32,1024]{4,3,1,0,2:T(8,128)(2,1)} %copy.38), calls=%async_computation | async-start | bytes 2097152 | tf_op jit(solution)/shard_map/all_to_all | solution.py:52
  19.5 1.0 constant_dynamic-slice_fusion
  20.5 0.0 all-gather.7.cloned.1.call-update
  22.4 3.2 %dynamic-slice_bitcast_fusion.1 = bf16[1024,1024]{1,0:T(8,128)(2,1)} fusion(bf16[2,2,1024,1024]{3,2,1,0:T(8,128)(2,1)} %param.6, s32[]{:T(128)S(6)} %select_n.12), kind=kLoop, calls=%fused_computation.32 | loop fusion | bytes 4194308 | tf_op jit(solution)/shard_map/squeeze | solution.py:11
  25.6 3.8 %fusion.47 = (bf16[1024,1024]{1,0:T(8,128)(2,1)}, bf16[1024,1024]{1,0:T(8,128)(2,1)}) fusion(bf16[2,2,1024,1024]{3,2,1,0:T(8,128)(2,1)} %param.6, s32[]{:T(128)S(6)} %select_n.12, s32[]{:T(128)S(6)} %add.15), kind=kLoop, calls=%fused_computation.62 | loop fusion | flops 1048576 | bytes 6291464 | tf_op jit(solution)/shard_map/neg | solution.py:12
  29.4 7.7 %all-to-all-done = bf16[2,1,8,32,1024]{4,3,1,0,2:T(8,128)(2,1)S(1)} async-done(((bf16[2,1,8,32,1024]{4,3,1,0,2:T(8,128)(2,1)}), bf16[2,1,8,32,1024]{4,3,1,0,2:T(8,128)(2,1)S(1)}, u32[]{:S(2)}, u32[]{:S(2)}) %all-to-all-start) | async-done | bytes 1048608 | tf_op jit(solution)/shard_map/all_to_all | solution.py:52
  37.1 3.2 %copy.39 = bf16[2,1,8,32,1024]{3,4,2,0,1:T(8,128)(2,1)} copy(bf16[2,1,8,32,1024]{4,3,1,0,2:T(8,128)(2,1)S(1)} %all-to-all-done) | data formatting | bytes 2097152 | tf_op jit(solution)/shard_map/all_to_all | solution.py:52
  40.3 3.9 %fusion.49 = (bf16[1,32,8,8,128]{1,2,4,3,0:T(8,128)(2,1)}, bf16[1,32,8,8,128]{1,2,4,3,0:T(8,128)(2,1)S(1)}) fusion(bf16[2,32,8,8,128]{1,2,4,3,0:T(8,128)(2,1)} %bitcast.74), kind=kLoop, calls=%fused_computation.64 | loop fusion | bytes 2097152 | tf_op jit(solution)/shard_map/slice | solution.py:17
  44.2 3.5 %copy.40 = bf16[1,32,8,8,128]{4,3,2,1,0:T(8,128)(2,1)S(1)} copy(bf16[1,32,8,8,128]{1,2,4,3,0:T(8,128)(2,1)} %get-tuple-element.9) | data formatting | bytes 1048576 | tf_op jit(solution)/shard_map/slice | solution.py:17
  47.7 2.0 copy.41
  49.7 0.2 copy_bitcast_fusion.4
  49.9 1.7 copy-done.4
  51.6 4.6 %fusion.30 = bf16[256,2048]{1,0:T(8,128)(2,1)S(1)} fusion(bf16[1024,1024]{1,0:T(8,128)(2,1)S(1)} %copy-done.4, bf16[1024,1024]{1,0:T(8,128)(2,1)} %get-tuple-element.5, bf16[1024,1024]{1,0:T(8,128)(2,1)} %get-tuple-element.6, bf16[256,1024]{1,0:T(8,128)(2,1)S(1)} %get-tuple-element.26, bf16[256,1024]{1,0:T(8,128)(2,1)S(1)} %get-tuple-element.27), kind=kOutput, calls=%fused_computation.26 | convolution fusion | flops 2183659520 | bytes 8388608 | tf_op jit(solution)/shard_map/dot_general | solution.py:18
  56.2 0.1 fusion.51
  56.3 0.1 pad_maximum_fusion
  56.4 52.9 %all_to_all.33 = bf16[2,8,1,32,1024]{4,3,2,0,1:T(8,128)(2,1)S(1)} all-to-all(bf16[2,8,1,32,1024]{4,3,2,0,1:T(8,128)(2,1)S(1)} %pad_maximum_fusion), channel_id=1, replica_groups=mesh['gx'=4,'gy'=2,'gz'=4] {'gy','gz'}, dimensions={1} | all-to-all | bytes 2097152 | tf_op jit(solution)/shard_map/all_to_all | solution.py:62
  109.4 3.2 %copy.44 = bf16[2,8,1,32,1024]{3,4,1,0,2:T(8,128)(2,1)} copy(bf16[2,8,1,32,1024]{4,3,2,0,1:T(8,128)(2,1)S(1)} %all_to_all.33) | data formatting | bytes 2097152 | tf_op jit(solution)/shard_map/all_to_all | solution.py:62
  112.5 3.9 %fusion.48 = (bf16[1,32,8,8,128]{1,2,4,3,0:T(8,128)(2,1)S(1)}, bf16[1,32,8,8,128]{1,2,4,3,0:T(8,128)(2,1)}) fusion(bf16[2,32,8,8,128]{1,2,4,3,0:T(8,128)(2,1)} %bitcast.75), kind=kLoop, calls=%fused_computation.63 | loop fusion | bytes 2097152 | tf_op jit(solution)/shard_map/slice | solution.py:29
  116.4 3.6 %copy.46 = bf16[1,32,8,8,128]{4,3,2,1,0:T(8,128)(2,1)S(1)} copy(bf16[1,32,8,8,128]{1,2,4,3,0:T(8,128)(2,1)} %get-tuple-element.8) | data formatting | bytes 1048576 | tf_op jit(solution)/shard_map/slice | solution.py:30
  120.1 0.1 copy.64
  120.2 2.0 copy.45
  122.2 1.0 copy.65
  123.2 1.9 fusion.45
  125.0 0.9 copy-done.3
  126.0 0.4 slice_bitcast_fusion.2
  126.4 0.6 copy-done.8
  127.0 2.4 fusion.27
  129.4 0.1 slice_bitcast_fusion.7
  129.5 0.1 pad_maximum_fusion.1
  129.6 1.2 copy.49
  130.8 3.8 %all-to-all-start.2 = ((bf16[2,1,32,8,8,128]{5,3,2,0,1,4:T(8,128)(2,1)}), bf16[2,1,32,8,8,128]{5,3,2,0,1,4:T(8,128)(2,1)S(1)}, u32[]{:S(2)}, u32[]{:S(2)}) async-start(bf16[2,1,32,8,8,128]{5,3,2,0,1,4:T(8,128)(2,1)} %copy.49), calls=%async_computation.2 | async-start | bytes 2097152 | tf_op jit(solution)/shard_map/all_to_all | solution.py:78
  134.6 78.8 %all-gather.7.cloned.1.call-done = bf16[1,2,1024,1024]{3,2,1,0:T(8,128)(2,1)} async-done(((bf16[1,2,256,1024]{3,2,1,0:T(8,128)(2,1)}), bf16[1,2,1024,1024]{3,2,1,0:T(8,128)(2,1)}) %all-gather.7.cloned.1.call-update) | async-done | bytes 4194320 | tf_op jit(solution)/shard_map/all_gather | solution.py:37
  213.4 3.2 %fusion.46 = bf16[1024,1024]{1,0:T(8,128)(2,1)} fusion(bf16[1,2,1024,1024]{3,2,1,0:T(8,128)(2,1)} %all-gather.7.cloned.1.call-done), kind=kLoop, calls=%fused_computation.61 | loop fusion | flops 1048576 | bytes 4194304 | tf_op jit(solution)/shard_map/neg | solution.py:12
  216.6 2.4 slice_bitcast_fusion
  219.0 0.0 all-to-all-done.2
  219.0 0.1 fusion.50
  219.1 0.1 copy.62
  219.2 0.1 copy.63
  219.3 1.3 copy-done.5
  220.6 0.6 copy-done.6
  221.3 19.6 %fusion.24 = bf16[256,2048]{1,0:T(8,128)(2,1)S(1)} fusion(bf16[1024,1024]{1,0:T(8,128)(2,1)} %get-tuple-element.14, bf16[1024,1024]{1,0:T(8,128)(2,1)S(1)} %copy-done.5, bf16[1024,1024]{1,0:T(8,128)(2,1)S(1)} %copy-done.6, bf16[256,1024]{1,0:T(8,128)(2,1)S(1)} %bitcast.88, bf16[256,1024]{1,0:T(8,128)(2,1)S(1)} %bitcast.89), kind=kOutput, calls=%fused_computation.24 | convolution fusion | flops 2183659520 | bytes 8388608 | tf_op jit(solution)/shard_map/dot_general | solution.py:32
  240.9 0.1 slice_bitcast_fusion.5
  241.0 1.1 pad_maximum_fusion.2
  (15 shorter events, 0.0 us)
Async XLA Ops:
  6.5 12.9 %copy-start = (bf16[2,2,256,1024]{3,2,1,0:T(8,128)(2,1)S(1)}, bf16[2,2,256,1024]{3,2,1,0:T(8,128)(2,1)}, u32[]{:S(2)}) copy-start(bf16[2,2,256,1024]{3,2,1,0:T(8,128)(2,1)} %param.8) | copy-start | bytes 6291460
  6.5 5.3 %copy-start.7 = (bf16[2,1,1,1,256,1024]{5,4,3,2,1,0:T(8,128)(2,1)S(1)}, bf16[2,1,1,1,256,1024]{5,4,3,2,1,0:T(8,128)(2,1)}, u32[]{:S(2)}) copy-start(bf16[2,1,1,1,256,1024]{5,4,3,2,1,0:T(8,128)(2,1)} %param.5) | copy-start | bytes 3145732
  6.5 116.6 %all-gather.5.cloned.1.call-start = ((), (), s32[]{:S(2)}) async-start(), calls=%async_computation.3 | async-start | bytes 4718592 | tf_op jit(solution)/shard_map/all_gather | solution.py:75
  13.0 24.2 %all-to-all-start = ((bf16[2,1,8,32,1024]{4,3,1,0,2:T(8,128)(2,1)}), bf16[2,1,8,32,1024]{4,3,1,0,2:T(8,128)(2,1)S(1)}, u32[]{:S(2)}, u32[]{:S(2)}) async-start(bf16[2,1,8,32,1024]{4,3,1,0,2:T(8,128)(2,1)} %copy.38), calls=%async_computation | async-start | bytes 2097152 | tf_op jit(solution)/shard_map/all_to_all | solution.py:52
  17.5 195.9 %all-gather.7.cloned.1.call-start = ((), (), s32[]{:S(2)}) async-start(), calls=%async_computation.4 | async-start | bytes 5242880 | tf_op jit(solution)/shard_map/all_gather | solution.py:37
  49.7 1.9 copy-start.4
  123.2 2.8 %copy-start.3 = (bf16[1,2,1024,1024]{3,2,1,0:T(8,128)(2,1)S(1)}, bf16[1,2,1024,1024]{3,2,1,0:T(8,128)(2,1)}, u32[]{:S(2)}) copy-start(bf16[1,2,1024,1024]{3,2,1,0:T(8,128)(2,1)} %all-gather.5.cloned.1.call-done) | copy-start | bytes 12582916
  126.0 1.0 copy-start.8
  130.8 88.2 %all-to-all-start.2 = ((bf16[2,1,32,8,8,128]{5,3,2,0,1,4:T(8,128)(2,1)}), bf16[2,1,32,8,8,128]{5,3,2,0,1,4:T(8,128)(2,1)S(1)}, u32[]{:S(2)}, u32[]{:S(2)}) async-start(bf16[2,1,32,8,8,128]{5,3,2,0,1,4:T(8,128)(2,1)} %copy.49), calls=%async_computation.2 | async-start | bytes 2097152 | tf_op jit(solution)/shard_map/all_to_all | solution.py:78
  213.4 3.2 %copy-start.2 = (bf16[1,2,1024,1024]{3,2,1,0:T(8,128)(2,1)S(1)}, bf16[1,2,1024,1024]{3,2,1,0:T(8,128)(2,1)}, u32[]{:S(2)}) copy-start(bf16[1,2,1024,1024]{3,2,1,0:T(8,128)(2,1)} %all-gather.7.cloned.1.call-done) | copy-start | bytes 12582916
  219.0 1.6 copy-start.5
  219.0 2.2 copy-start.6
  221.3 20.8 %copy-start.1 = (bf16[2,2,256,1024]{3,2,1,0:T(8,128)(2,1)S(1)}, bf16[2,2,256,1024]{3,2,1,0:T(8,128)(2,1)}, u32[]{:S(2)}) copy-start(bf16[2,2,256,1024]{3,2,1,0:T(8,128)(2,1)} %param.8) | copy-start | bytes 6291460
Sparse Core Ops, SparseCore 0:
  11.9 97.4 all-gather.4
  111.0 102.3 all-gather.6
where the time goes:
time: 251 us; the launch traced here: 249 us
  waiting for transfers between devices  86.5 us (34%)
  blocking collectives  52.9 us (21%)
  local copies, waits for them, and re-layouts  45 us (18%)
  matrix products  26.6 us (11%)
  between operations  19.3 us (8%)
  other arithmetic  10.2 us (4%)
  starting transfers between devices  8.32 us (3%)
    all_gather x1, waiting for transfers between devices, third_contraction(): lax.all_gather(local_third, 'gz', axis=1, tiled=True)  78.8 us
    all_to_all x1, blocking collectives, body(): lax.all_to_all(middle.reshape(2, group_two, 1, rows_two, WIDTH), ('gy', '...  52.9 us
    dot_general x2, matrix products, make_accumulate(): jnp.dot(joined, complex_matrix(shard_rows), preferred_element_type=jnp.fl...  22 us
    slice x3, local copies, waits for them, and re-layouts, complex_product(): joined = jnp.concatenate([operand[0], operand[1]], axis=1)  9.4 us
    neg x3, other arithmetic, complex_matrix(): bottom_half = jnp.concatenate([-branch[1], branch[0]], axis=1)  8.94 us
    all_to_all x1, waiting for transfers between devices, body(): lax.all_to_all(stem.reshape(2, 1, group_one, rows_one, WIDTH), ('gx', 'gy...  7.71 us
    unnamed x22, local copies, waits for them, and re-layouts  6.45 us
    squeeze x3, local copies, waits for them, and re-layouts, complex_matrix(): top_half = jnp.concatenate([branch[0], branch[1]], axis=1)  6.02 us
  transfers between devices with their start and end apart: 4, of which 2 were waited for; matrix products, arithmetic and copies ran while one was open for 21% of the time, Pallas kernels for 0%

commit v1 on v0

--- a/solution.py
+++ b/solution.py
@@ -1,6 +1,10 @@
+import functools
+
 import jax
 import jax.numpy as jnp
 from jax import lax
+from jax.experimental import pallas as pl
+from jax.experimental.pallas import tpu as pltpu
 from jax.sharding import PartitionSpec as P
 
 WIDTH = 1024
@@ -86,9 +90,322 @@
     return result.reshape(stem.shape)
 
 
+MESH = pl.DeviceIdType.MESH
+VMEM_LIMIT = 56 * 1024 * 1024
+TILE = 256
+LANE = 128
+
+
+def complex_tile(lhs, rhs):
+    result = jnp.dot(lhs, rhs, preferred_element_type=jnp.float32)
+    m, n = result.shape[0] // 2, result.shape[1] // 2
+    real = result[:m, :n] - result[m:, n:]
+    imag = result[m:, :n] + result[:m, n:]
+    return real.astype(jnp.bfloat16), imag.astype(jnp.bfloat16)
+
+
+def kernel(
+    dims, slices, stem, one_hbm, two_in, three_in, out,
+    perm, one, one_perm, two, three, sorted_stem, first, second, third, result,
+    one_sem, own_sem, stem_send, stem_recv, part_send, part_recv, back_send, back_recv,
+):
+    nx, ny, nz = dims
+    group = ny * nz
+    devices = nx * group
+    gx, gy, gz = lax.axis_index("gx"), lax.axis_index("gy"), lax.axis_index("gz")
+    line, core = gx // 2, gx % 2
+    me = (gx * ny + gy) * nz + gz
+    place = gy * nz + gz
+
+    load_one = pltpu.make_async_copy(one_hbm, one, one_sem)
+    load_one.start()
+
+    def coordinates(index):
+        return (index // group, (index // nz) % ny, index % nz)
+
+    barrier = pltpu.get_barrier_semaphore()
+
+    def greet(step, carry):
+        pl.semaphore_signal(
+            barrier, inc=1, device_id=coordinates((me + step) % devices), device_id_type=MESH
+        )
+        return carry
+
+    lax.fori_loop(1, devices, greet, 0)
+
+    rows_two, rows_three = WIDTH // group, WIDTH // nz
+    piece = rows_two // nx
+    two[:, pl.ds(pl.multiple_of(place * rows_two, rows_two), rows_two), :] = two_in[slices[1]]
+    three[:, pl.ds(pl.multiple_of(gz * rows_three, rows_three), rows_three), :] = three_in[slices[2]]
+
+    def make_perm(tile, carry):
+        column = lax.broadcasted_iota(jnp.int32, (WIDTH, TILE), 1) + tile * TILE
+        row = lax.broadcasted_iota(jnp.int32, (WIDTH, TILE), 0)
+        wanted = (column % LANE) * group + column // LANE
+        perm[tile] = jnp.where(row == wanted, 1.0, 0.0).astype(jnp.bfloat16)
+        return carry
+
+    lax.fori_loop(0, WIDTH // TILE, make_perm, 0)
+    pl.semaphore_wait(barrier, devices - 1)
+
+    sends = []
+
+    def piece_two_of(line_of, x, back):
+        start = (x * nz + (gz + nz - back) % nz) * rows_two + (line_of * 2 + core) * piece
+        return two.at[:, pl.ds(pl.multiple_of(start, piece), piece), :]
+
+    def piece_three_of(line_of, x, back):
+        start = ((gz + nz - back) % nz) * rows_three + ((line_of * 2 + core) * ny + x) * piece
+        return three.at[:, pl.ds(pl.multiple_of(start, piece), piece), :]
+
+    def send(ref, device):
+        index = len(sends)
+        copy = pltpu.make_async_remote_copy(
+            src_ref=ref, dst_ref=ref,
+            send_sem=part_send.at[index], recv_sem=part_recv.at[index],
+            device_id=device, device_id_type=MESH,
+        )
+        copy.start()
+        sends.append(copy)
+        return copy
+
+    other_line, other_x = 1 - line, 1 - gy
+    to_line = (other_line * 2 + core, gy, gz)
+    to_x = (gx, other_x, gz)
+    to_core = (line * 2 + 1 - core, gy, gz)
+
+    two_z, three_z = {}, {}
+    for step in range(1, nz):
+        device = (gx, gy, (gz + step) % nz)
+        two_z[step] = send(piece_two_of(line, gy, 0), device)
+        three_z[step] = send(piece_three_of(line, gy, 0), device)
+    two_x = {0: send(piece_two_of(line, gy, 0), to_x)}
+
+    def sort_stem(tile, carry):
+        operand = stem[...].reshape(2 * ROWS, WIDTH)
+        moved = jnp.dot(operand, perm[tile], preferred_element_type=jnp.float32)
+        moved = moved.astype(jnp.bfloat16).reshape(2, ROWS, TILE)
+        sorted_stem[:, :, pl.ds(pl.multiple_of(tile * TILE, TILE), TILE)] = moved
+        return carry
+
+    lax.fori_loop(0, WIDTH // TILE, sort_stem, 0)
+    rows_one = ROWS // nx
+
+    def stem_block(index):
+        return sorted_stem.at[
+            :,
+            pl.ds(pl.multiple_of((index // group) * rows_one, rows_one), rows_one),
+            pl.ds(pl.multiple_of((index % group) * LANE, LANE), LANE),
+        ]
+
+    def landing(index):
+        return first.at[:, index % nz, :, pl.ds(pl.multiple_of((index // nz) * LANE, LANE), LANE)]
+
+    def stem_copy(step):
+        target = (me + step) % devices
+        return pltpu.make_async_remote_copy(
+            src_ref=stem_block(target), dst_ref=landing(me),
+            send_sem=stem_send.at[step], recv_sem=stem_recv.at[step],
+            device_id=coordinates(target), device_id_type=MESH,
+        )
+
+    def send_stem(step, carry):
+        stem_copy(step).start()
+        return carry
+
+    lax.fori_loop(1, devices, send_stem, 0)
+    own = pltpu.make_async_copy(stem_block(me), landing(me), own_sem.at[0])
+    own.start()
+
+    load_one.wait()
+
+    def sort_one(tile, carry):
+        for part in range(2):
+            moved = jnp.dot(
+                one[slices[0], part], perm[tile], preferred_element_type=jnp.float32
+            ).astype(jnp.bfloat16)
+            for half in range(2):
+                one_perm[2 * tile + half, :, part * LANE : (part + 1) * LANE] = moved[
+                    :, half * LANE : (half + 1) * LANE
+                ]
+        return carry
+
+    lax.fori_loop(0, WIDTH // TILE, sort_one, 0)
+
+    two_y, three_y, three_x = {}, {}, {}
+    two_core, three_core = [], []
+    for step in range(1, nz):
+        two_z[step].wait_recv()
+        two_x[step] = send(piece_two_of(line, gy, step), to_x)
+        three_z[step].wait_recv()
+        three_y[step] = send(piece_three_of(line, gy, step), to_line)
+    for step in range(1, nz):
+        two_y[0, step] = send(piece_two_of(line, gy, step), to_line)
+        three_x[0, step] = send(piece_three_of(line, gy, step), to_x)
+        two_core.append(send(piece_two_of(line, gy, step), to_core))
+        three_core.append(send(piece_three_of(line, gy, step), to_core))
+    for step in range(nz):
+        two_x[step].wait_recv()
+        two_y[1, step] = send(piece_two_of(line, other_x, step), to_line)
+        two_core.append(send(piece_two_of(line, other_x, step), to_core))
+        if step > 0:
+            three_y[step].wait_recv()
+            three_x[1, step] = send(piece_three_of(other_line, gy, step), to_x)
+            three_core.append(send(piece_three_of(other_line, gy, step), to_core))
+
+    own.wait()
+
+    def await_stem(step, carry):
+        stem_copy(step).wait_recv()
+        return carry
+
+    lax.fori_loop(1, devices, await_stem, 0)
+    chunk = ROWS // group
+
+    def contract_first(k, carry):
+        operand = first[...].reshape(2 * ROWS, WIDTH)
+        for part, value in enumerate(complex_tile(operand, one_perm[k])):
+            for c in range(nz):
+                for ry in range(ny):
+                    row, column = (c * ny + ry) * chunk, (ry * nz + c) * LANE
+                    second[part, k, :, column : column + LANE] = value[row : row + chunk]
+        return carry
+
+    lax.fori_loop(0, group, contract_first, 0)
+
+    for step in range(1, nz):
+        two_y[0, step].wait_recv()
+        two_core.append(send(piece_two_of(other_line, gy, step), to_core))
+        three_x[0, step].wait_recv()
+        three_core.append(send(piece_three_of(line, other_x, step), to_core))
+    for step in range(nz):
+        two_y[1, step].wait_recv()
+        two_core.append(send(piece_two_of(other_line, other_x, step), to_core))
+        if step > 0:
+            three_x[1, step].wait_recv()
+            three_core.append(send(piece_three_of(other_line, other_x, step), to_core))
+
+    for copy in two_core:
+        copy.wait_recv()
+
+    def contract_second(s, carry):
+        operand = second[...].reshape(2 * ROWS, WIDTH)
+        columns = pl.ds(pl.multiple_of(s * LANE, LANE), LANE)
+        branch = jnp.concatenate([two[0, :, columns], two[1, :, columns]], axis=1)
+        for part, value in enumerate(complex_tile(operand, branch)):
+            for k in range(group):
+                third[part, s, :, k * LANE : (k + 1) * LANE] = value[k * chunk : (k + 1) * chunk]
+        return carry
+
+    lax.fori_loop(0, group, contract_second, 0)
+
+    for copy in three_core:
+        copy.wait_recv()
+    tiles = WIDTH // TILE
+
+    def back_copy(tile, step):
+        target = (place + step) % group
+        columns = pl.ds(pl.multiple_of(tile * TILE, TILE), TILE)
+        return pltpu.make_async_remote_copy(
+            src_ref=result.at[target, :, :, columns], dst_ref=out.at[place, :, :, columns],
+            send_sem=back_send.at[tile, step], recv_sem=back_recv.at[tile, step],
+            device_id=(gx, target // nz, target % nz), device_id_type=MESH,
+        )
+
+    def contract_third(tile, carry):
+        operand = third[...].reshape(2 * ROWS, WIDTH)
+        columns = pl.ds(pl.multiple_of(tile * TILE, TILE), TILE)
+        branch = jnp.concatenate([three[0, :, columns], three[1, :, columns]], axis=1)
+        for part, value in enumerate(complex_tile(operand, branch)):
+            result[:, part, :, columns] = value.reshape(group, chunk, TILE)
+
+        def send_back(step, inner):
+            back_copy(tile, step).start()
+            return inner
+
+        lax.fori_loop(1, group, send_back, 0)
+        return carry
+
+    lax.fori_loop(0, tiles, contract_third, 0)
+    keep = pltpu.make_async_copy(result.at[place], out.at[place], own_sem.at[1])
+    keep.start()
+    keep.wait()
+
+    for copy in sends:
+        copy.wait_send()
+
+    def end_stem(step, carry):
+        stem_copy(step).wait_send()
+        return carry
+
+    lax.fori_loop(1, devices, end_stem, 0)
+
+    def end_back(index, carry):
+        copy = back_copy(index // (group - 1), index % (group - 1) + 1)
+        copy.wait_send()
+        copy.wait_recv()
+        return carry
+
+    lax.fori_loop(0, tiles * (group - 1), end_back, 0)
+
+
+def fused_body(dims, stem, branch_one, branch_two, branch_three, slice_values):
+    nx, ny, nz = dims
+    group = ny * nz
+    devices = nx * group
+    chunk = ROWS // group
+    pieces = 2 * (nz - 1) + nz + (nz - 1) + (2 * nz - 1) + 2 * (nz - 1)
+    pieces = pieces + 2 * (2 * nz - 1) + 4 * (nz - 1)
+    bf16 = jnp.bfloat16
+    vmem = pl.BlockSpec(memory_space=pltpu.VMEM)
+    dma = pltpu.SemaphoreType.DMA
+    blocks = pl.pallas_call(
+        functools.partial(kernel, dims),
+        out_shape=jax.ShapeDtypeStruct((group, 2, chunk, WIDTH), bf16),
+        in_specs=[
+            pl.BlockSpec(memory_space=pltpu.SMEM),
+            vmem,
+            pl.BlockSpec(memory_space=pl.ANY),
+            vmem,
+            vmem,
+        ],
+        out_specs=pl.BlockSpec(memory_space=pl.ANY),
+        scratch_shapes=[
+            pltpu.VMEM((WIDTH // TILE, WIDTH, TILE), bf16),
+            pltpu.VMEM(branch_one.shape, bf16),
+            pltpu.VMEM((group, WIDTH, 2 * LANE), bf16),
+            pltpu.VMEM((2, WIDTH, WIDTH), bf16),
+            pltpu.VMEM((2, WIDTH, WIDTH), bf16),
+            pltpu.VMEM((2, ROWS, WIDTH), bf16),
+            pltpu.VMEM((2, nz, ROWS // nx, WIDTH), bf16),
+            pltpu.VMEM((2, group, chunk, WIDTH), bf16),
+            pltpu.VMEM((2, group, chunk, WIDTH), bf16),
+            pltpu.VMEM((group, 2, chunk, WIDTH), bf16),
+            dma,
+            dma((2,)),
+            dma((devices,)),
+            dma((devices,)),
+            dma((pieces,)),
+            dma((pieces,)),
+            dma((WIDTH // TILE, group)),
+            dma((WIDTH // TILE, group)),
+        ],
+        compiler_params=pltpu.CompilerParams(
+            collective_id=0, has_side_effects=True, vmem_limit_bytes=VMEM_LIMIT
+        ),
+        cost_estimate=pl.CostEstimate(
+            flops=24 * ROWS * WIDTH * WIDTH, bytes_accessed=16 * WIDTH * WIDTH, transcendentals=0
+        ),
+    )(slice_values, stem.reshape(2, ROWS, WIDTH), branch_one, branch_two, branch_three)
+    return blocks.transpose(1, 2, 0, 3).reshape(stem.shape)
+
+
 def solution(mesh):
+    dims = (mesh.shape["gx"], mesh.shape["gy"], mesh.shape["gz"])
+    group_one, group_two = dims[0] * dims[1], dims[1] * dims[2]
+    fused = group_one == group_two == WIDTH // LANE and dims[0] == 4 and dims[1] == 2
     return jax.shard_map(
-        body,
+        functools.partial(fused_body, dims) if fused else body,
         mesh=mesh,
         in_specs=(
             P(None, "gx", "gy", "gz", None, None),

time: 251 us -> 99.9 us (0.40)
  Pallas kernels: 0 us -> 97 us
  waiting for transfers between devices: 86.5 us -> 0 us
  blocking collectives: 52.9 us -> 0 us
  local copies, waits for them, and re-layouts: 45 us -> 2.77 us
  matrix products: 26.6 us -> 0 us
  between operations: 19.3 us -> 0.01 us
  other arithmetic: 10.2 us -> 0 us
  starting transfers between devices: 8.32 us -> 0 us
    pallas_call x0 -> x1, Pallas kernels: none -> 97 us  [fused_body(): pl.pallas_call(functools.partial(kernel, dims), out_shape=jax.ShapeDtypeS...]
    all_gather x2 -> x0, waiting for transfers between devices: 78.8 us -> none  [the longest x1 78.8 us: third_contraction(): lax.all_gather(local_third, 'gz', axis=1, tiled=True)]
    all_to_all x1 -> x0, blocking collectives: 52.9 us -> none  [body(): lax.all_to_all(middle.reshape(2, group_two, 1, rows_two, WIDTH), ('gy', '...]
    dot_general x3 -> x0, matrix products: 26.6 us -> none  [the longest x2 22 us: make_accumulate(): jnp.dot(joined, complex_matrix(shard_rows), preferred_element_type=jnp.fl...]
    slice x9 -> x0, local copies, waits for them, and re-layouts: 20.6 us -> none  [the longest x3 9.4 us: complex_product(): joined = jnp.concatenate([operand[0], operand[1]], axis=1)]
    neg x3 -> x0, other arithmetic: 8.94 us -> none  [complex_matrix(): bottom_half = jnp.concatenate([-branch[1], branch[0]], axis=1)]
    all_to_all x2 -> x0, starting transfers between devices: 8.32 us -> none  [the longest x1 4.54 us: body(): lax.all_to_all(stem.reshape(2, 1, group_one, rows_one, WIDTH), ('gx', 'gy...]
    all_to_all x2 -> x0, waiting for transfers between devices: 7.72 us -> none  [the longest x1 7.71 us: body(): lax.all_to_all(stem.reshape(2, 1, group_one, rows_one, WIDTH), ('gx', 'gy...]
  transfers between devices with their start and end apart: 4 -> 0, of which waited for: 2 -> 0; matrix products, arithmetic and copies ran while one was open for 21% -> 0% of each run, Pallas kernels for 0% -> 0%
where the time goes in v1:
time: 99.9 us; the launch traced here: 99.8 us
  Pallas kernels  97 us (97%)
  local copies, waits for them, and re-layouts  2.77 us (3%)
    pallas_call x1, Pallas kernels, fused_body(): pl.pallas_call(functools.partial(kernel, dims), out_shape=jax.ShapeDtypeS...  97 us
    transpose x1, local copies, waits for them, and re-layouts, fused_body(): return blocks.transpose(1, 2, 0, 3).reshape(stem.shape)  2.77 us

profile of v1, /device:TPU:5, one launch (start us, length us, event | category | flops | bytes accessed | tf_op | source)
XLA Modules:
  0.0 99.8 jit_solution(18024862194377193813)
XLA Ops:
  0.0 97.0 %shard_map.55 = bf16[8,2,32,1024]{3,2,1,0:T(8,128)(2,1)} custom-call(s32[3]{0:T(128)} %slices.1, bf16[2,256,1024]{2,1,0:T(8,128)(2,1)} %bitcast.8, bf16[2,2,1024,1024]{3,2,1,0:T(8,128)(2,1)} %one_hbm.1, bf16[2,2,128,1024]{3,2,1,0:T(8,128)(2,1)} %two_in.1, bf16[2,2,256,1024]{3,2,1,0:T(8,128)(2,1)} %three_in.1), custom_call_target="tpu_custom_call" | custom-call | flops 6442450944 | bytes 16777216 | tf_op jit(solution)/shard_map/pallas_call | solution.py:362
  97.0 2.8 %copy.9 = bf16[2,32,8,1024]{3,2,1,0:T(8,128)(2,1)} copy(bf16[2,32,8,1024]{3,1,0,2:T(8,128)(2,1)} %bitcast.7) | data formatting | bytes 2097152 | tf_op jit(solution)/shard_map/transpose | solution.py:400

commit v2 on v1

--- a/solution.py
+++ b/solution.py
@@ -107,7 +107,7 @@
 def kernel(
     dims, slices, stem, one_hbm, two_in, three_in, out,
     perm, one, one_perm, two, three, sorted_stem, first, second, third, result,
-    one_sem, own_sem, stem_send, stem_recv, part_send, part_recv, back_send, back_recv,
+    one_sem, own_sem, stem_send, stem_recv, part_send, part_recv, z_send, z_recv, back_send, back_recv,
 ):
     nx, ny, nz = dims
     group = ny * nz
@@ -150,12 +150,21 @@
 
     sends = []
 
+    upper = gz // 2
+    depth = gz + upper * (nz - 1 - 2 * gz)
+
+    def mirrored(position):
+        return position + upper * (nz - 1 - 2 * position)
+
+    def z_of(back):
+        return gz if back == 0 else mirrored(1 - depth if back == 1 else back)
+
     def piece_two_of(line_of, x, back):
-        start = (x * nz + (gz + nz - back) % nz) * rows_two + (line_of * 2 + core) * piece
+        start = (x * nz + z_of(back)) * rows_two + (line_of * 2 + core) * piece
         return two.at[:, pl.ds(pl.multiple_of(start, piece), piece), :]
 
     def piece_three_of(line_of, x, back):
-        start = ((gz + nz - back) % nz) * rows_three + ((line_of * 2 + core) * ny + x) * piece
+        start = z_of(back) * rows_three + ((line_of * 2 + core) * ny + x) * piece
         return three.at[:, pl.ds(pl.multiple_of(start, piece), piece), :]
 
     def send(ref, device):
@@ -174,11 +183,38 @@
     to_x = (gx, other_x, gz)
     to_core = (line * 2 + 1 - core, gy, gz)
 
-    two_z, three_z = {}, {}
-    for step in range(1, nz):
-        device = (gx, gy, (gz + step) % nz)
-        two_z[step] = send(piece_two_of(line, gy, 0), device)
-        three_z[step] = send(piece_three_of(line, gy, 0), device)
+    pieces_of = (piece_two_of, piece_three_of)
+
+    def z_copy(kind, back, hop, position):
+        ref = pieces_of[kind](line, gy, back)
+        return pltpu.make_async_remote_copy(
+            src_ref=ref, dst_ref=ref,
+            send_sem=z_send.at[kind, hop], recv_sem=z_recv.at[kind, z_of(back)],
+            device_id=(gx, gy, mirrored(position)), device_id_type=MESH,
+        )
+
+    def z_hops(back):
+        return [z_copy(kind, back, 1 + back, 2 if back < 2 else 0) for kind in range(2)]
+
+    for kind in range(2):
+        z_copy(kind, 0, 0, 1 - depth).start()
+
+    @pl.when(depth == 1)
+    def _():
+        for copy in z_hops(0):
+            copy.start()
+
+    def pass_on(back):
+        for kind in range(2):
+            z_copy(kind, back, 0, 0).wait_recv()
+
+        @pl.when(depth == 1)
+        def _():
+            for copy in z_hops(back):
+                copy.start()
+
+    two_y, three_y, three_x = {}, {}, {}
+    two_core, three_core = [], []
     two_x = {0: send(piece_two_of(line, gy, 0), to_x)}
 
     def sort_stem(tile, carry):
@@ -209,13 +245,29 @@
             device_id=coordinates(target), device_id_type=MESH,
         )
 
-    def send_stem(step, carry):
-        stem_copy(step).start()
-        return carry
-
-    lax.fori_loop(1, devices, send_stem, 0)
+    def send_plane(step, carry):
+        stem_copy(step * nz).start()
+        return carry
+
+    def send_stem_rest(step, carry):
+        stem_copy(step + step // (nz - 1) + 1).start()
+        return carry
+
+    lax.fori_loop(1, devices // nz, send_plane, 0)
     own = pltpu.make_async_copy(stem_block(me), landing(me), own_sem.at[0])
     own.start()
+
+    for step in range(1, nz):
+        pass_on(step)
+        two_x[step] = send(piece_two_of(line, gy, step), to_x)
+        three_y[step] = send(piece_three_of(line, gy, step), to_line)
+    for step in range(1, nz):
+        two_y[0, step] = send(piece_two_of(line, gy, step), to_line)
+        three_x[0, step] = send(piece_three_of(line, gy, step), to_x)
+    lax.fori_loop(0, devices - devices // nz, send_stem_rest, 0)
+    for step in range(1, nz):
+        two_core.append(send(piece_two_of(line, gy, step), to_core))
+        three_core.append(send(piece_three_of(line, gy, step), to_core))
 
     load_one.wait()
 
@@ -232,18 +284,6 @@
 
     lax.fori_loop(0, WIDTH // TILE, sort_one, 0)
 
-    two_y, three_y, three_x = {}, {}, {}
-    two_core, three_core = [], []
-    for step in range(1, nz):
-        two_z[step].wait_recv()
-        two_x[step] = send(piece_two_of(line, gy, step), to_x)
-        three_z[step].wait_recv()
-        three_y[step] = send(piece_three_of(line, gy, step), to_line)
-    for step in range(1, nz):
-        two_y[0, step] = send(piece_two_of(line, gy, step), to_line)
-        three_x[0, step] = send(piece_three_of(line, gy, step), to_x)
-        two_core.append(send(piece_two_of(line, gy, step), to_core))
-        three_core.append(send(piece_three_of(line, gy, step), to_core))
     for step in range(nz):
         two_x[step].wait_recv()
         two_y[1, step] = send(piece_two_of(line, other_x, step), to_line)
@@ -333,6 +373,14 @@
 
     for copy in sends:
         copy.wait_send()
+    for kind in range(2):
+        z_copy(kind, 0, 0, 1 - depth).wait_send()
+
+    @pl.when(depth == 1)
+    def _():
+        for back in range(nz):
+            for copy in z_hops(back):
+                copy.wait_send()
 
     def end_stem(step, carry):
         stem_copy(step).wait_send()
@@ -354,7 +402,7 @@
     group = ny * nz
     devices = nx * group
     chunk = ROWS // group
-    pieces = 2 * (nz - 1) + nz + (nz - 1) + (2 * nz - 1) + 2 * (nz - 1)
+    pieces = nz + (nz - 1) + (2 * nz - 1) + 2 * (nz - 1)
     pieces = pieces + 2 * (2 * nz - 1) + 4 * (nz - 1)
     bf16 = jnp.bfloat16
     vmem = pl.BlockSpec(memory_space=pltpu.VMEM)
@@ -387,6 +435,8 @@
             dma((devices,)),
             dma((pieces,)),
             dma((pieces,)),
+            dma((2, nz + 1)),
+            dma((2, nz)),
             dma((WIDTH // TILE, group)),
             dma((WIDTH // TILE, group)),
         ],
@@ -403,7 +453,7 @@
 def solution(mesh):
     dims = (mesh.shape["gx"], mesh.shape["gy"], mesh.shape["gz"])
     group_one, group_two = dims[0] * dims[1], dims[1] * dims[2]
-    fused = group_one == group_two == WIDTH // LANE and dims[0] == 4 and dims[1] == 2
+    fused = group_one == group_two == WIDTH // LANE and dims == (4, 2, 4)
     return jax.shard_map(
         functools.partial(fused_body, dims) if fused else body,
         mesh=mesh,

time: 99.9 us -> 91.9 us (0.920)
  Pallas kernels: 97 us -> 89 us
    pallas_call x1, Pallas kernels: 97 us -> 89 us  [fused_body(): pl.pallas_call(functools.partial(kernel, dims), out_shape=jax.ShapeDtypeS...]
where the time goes in v2:
time: 91.9 us; the launch traced here: 91.8 us
  Pallas kernels  89 us (97%)
  local copies, waits for them, and re-layouts  2.77 us (3%)
    pallas_call x1, Pallas kernels, fused_body(): pl.pallas_call(functools.partial(kernel, dims), out_shape=jax.ShapeDtypeS...  89 us
    transpose x1, local copies, waits for them, and re-layouts, fused_body(): return blocks.transpose(1, 2, 0, 3).reshape(stem.shape)  2.77 us

profile of v2, /device:TPU:5, one launch (start us, length us, event | category | flops | bytes accessed | tf_op | source)
XLA Modules:
  0.0 91.8 jit_solution(16377448410785130564)
XLA Ops:
  0.0 89.0 %shard_map.55 = bf16[8,2,32,1024]{3,2,1,0:T(8,128)(2,1)} custom-call(s32[3]{0:T(128)} %slices.1, bf16[2,256,1024]{2,1,0:T(8,128)(2,1)} %bitcast.8, bf16[2,2,1024,1024]{3,2,1,0:T(8,128)(2,1)} %one_hbm.1, bf16[2,2,128,1024]{3,2,1,0:T(8,128)(2,1)} %two_in.1, bf16[2,2,256,1024]{3,2,1,0:T(8,128)(2,1)} %three_in.1), custom_call_target="tpu_custom_call" | custom-call | flops 6442450944 | bytes 16777216 | tf_op jit(solution)/shard_map/pallas_call | solution.py:410
  89.0 2.8 %copy.9 = bf16[2,32,8,1024]{3,2,1,0:T(8,128)(2,1)} copy(bf16[2,32,8,1024]{3,1,0,2:T(8,128)(2,1)} %bitcast.7) | data formatting | bytes 2097152 | tf_op jit(solution)/shard_map/transpose | solution.py:450
